TPU v7x, 32 devices: a whole 2x2x4 slice. The times are simulated.
32 devices in a mesh: chan: 16 (over z, y, core), loc: 2 (over x).
Axes of the slice: x: 2, y: 2, z: 4, core: 2. Of those that a mesh axis runs over, the one named last changes fastest.
Arguments:
- pixels: bfloat16 [512, 256, 256], P('loc', 'chan'), may hold values from -6 to 6
- patch_mask: int32 [512, 256], P('loc', 'chan'), may hold values 0 or 1
- group_map: int32 [256], replicated, may hold values from 0 to 63, as said below
- embed_weight: bfloat16 [256, 2048], P(None, 'loc'), may hold values from -0.375 to 0.375
- mask_token: bfloat16 [2048], replicated, may hold values from -6 to 6
- chan_embed: bfloat16 [256, 2048], P('chan'), may hold values from -3 to 3
- agg_weight: float32 [256], P('chan'), may hold values from 0.5 to 2
- query_key: bfloat16 [16, 2048], replicated, may hold values from -0.02734375 to 0.02734375
- group_bias: float32 [16, 64], replicated, may hold values from -0.5 to 255
- norm_gain: float32 [2048], replicated, may hold values from 0.25 to 1.75
- head_weight: bfloat16 [2048, 256, 256], P(None, 'chan'), may hold values from -0.125 to 0.125
- head_bias: float32 [256, 256], P('chan'), may hold values from -3 to 3
Outputs:
- rebuilt: bfloat16 [512, 256, 256], P('loc', 'chan')
Inputs may be any that keep to these rules, and one draw needn't show every extreme that they name: `group_map`: the 4 channels of each bundle (channels k * 4 to k * 4 + 3) name at most two distinct groups.
All inputs are finite; a program needn't handle non-finite values. No bound on the sum of `patch_mask` on one device may be relied on, other than what follows from the above.
Results may differ from a plain program's by a relative error of at most 0.0051.
Values may be sent and summed in bfloat16 or wider, within the bound.
No kernel may reach another device: no remote copies, remote signals or barrier semaphores. Data moves between devices by JAX's collectives and lax.ppermute only.
A program may use at most 128 MiB of HBM per device.

v0:
```python
import functools

import jax
import jax.numpy as jnp
from jax import lax
from jax.experimental import pallas as pl
from jax.experimental.pallas import tpu as pltpu
from jax.sharding import PartitionSpec as P

G = 64
BUNDLE = 4
LANES = 128
VMEM = pl.BlockSpec(memory_space=pltpu.VMEM)
ANY = pl.BlockSpec(memory_space=pl.ANY)
F32, BF16 = jnp.float32, jnp.bfloat16


def dot(left, right, left_dim=1, right_dim=0):
    dims = (((left_dim,), (right_dim,)), ((), ()))
    return lax.dot_general(left, right, dims, preferred_element_type=F32)


def iota(shape, axis):
    return lax.broadcasted_iota(jnp.int32, shape, axis)


def halves(value):
    high = value.astype(BF16)
    return high, (value - high.astype(F32)).astype(BF16)


def gelu(value):
    return 0.5 * value * (1.0 + lax.erf(value * 0.7071067811865476))


def slot_tables(group_map):
    bundled = group_map.reshape(-1, BUNDLE)
    lowest = jnp.min(bundled, axis=1)
    highest = jnp.max(bundled, axis=1)
    slot_index = (bundled != lowest[:, None]).astype(jnp.int32)
    choose = slot_index[:, None, :] == jnp.arange(2, dtype=jnp.int32)[None, :, None]
    slot_group = jnp.stack([lowest, highest], axis=1).reshape(-1)
    to_group = jnp.arange(G, dtype=jnp.int32)[:, None] == slot_group[None, :]
    return (choose.astype(BF16), to_group.astype(BF16))


def attend(aggregate, query_key, group_bias, norm_gain):
    rows, _, features = aggregate.shape
    heads = query_key.shape[0]
    high = lax.Precision.HIGHEST
    scores = jnp.einsum("lge,he->lhg", aggregate, query_key.astype(F32), precision=high)
    weights = jax.nn.softmax(scores + group_bias[None], axis=-1)
    split = aggregate.reshape(rows, G, heads, features // heads)
    pooled = jnp.einsum("lhg,lghd->lhd", weights, split, precision=high).reshape(rows, features)
    inverse_rms = lax.rsqrt(jnp.mean(pooled * pooled, axis=-1, keepdims=True) + 1e-06)
    return (pooled * inverse_rms * norm_gain[None]).astype(BF16)


def plain_join(
    pixels, patch_mask, group_map, embed_weight, mask_token, chan_embed, agg_weight, query_key, group_bias, norm_gain
):
    pixel_count = pixels.shape[2]
    choose, to_group = slot_tables(group_map)
    source_pixels = lax.all_to_all(pixels, "chan", split_axis=0, concat_axis=1, tiled=True)
    source_mask = lax.all_to_all(patch_mask, "chan", split_axis=0, concat_axis=1, tiled=True)
    offsets = lax.all_gather(chan_embed, "chan", axis=0, tiled=True).astype(F32)
    weights = lax.all_gather(agg_weight, "chan", axis=0, tiled=True)
    section = lax.all_gather(embed_weight, "loc", axis=1, tiled=True)
    rows, channels, _ = source_pixels.shape
    features = section.shape[1]
    projected = jnp.dot(source_pixels.reshape(rows * channels, pixel_count), section, preferred_element_type=F32)
    projected = projected.reshape(rows, channels, features)
    hidden = source_mask.reshape(rows, channels, 1) == 1
    pre = jnp.where(hidden, mask_token.astype(F32)[None, None, :], projected) + offsets[None]
    weighted = (jax.nn.gelu(pre, approximate=False) * weights[None, :, None]).astype(BF16)
    bundled = weighted.reshape(rows, channels // BUNDLE, BUNDLE, features)
    sums = jnp.einsum("lbke,bsk->lbse", bundled, choose, preferred_element_type=F32)
    sums = sums.reshape(rows, channels // BUNDLE * 2, features).astype(BF16)
    aggregate = jnp.einsum("gq,lqe->lge", to_group, sums, preferred_element_type=F32)
    return attend(aggregate, query_key, group_bias, norm_gain)


def plain_shards(
    pixels,
    patch_mask,
    group_map,
    embed_weight,
    mask_token,
    chan_embed,
    agg_weight,
    query_key,
    group_bias,
    norm_gain,
    head_weight,
    head_bias,
):
    _, own_channels, pixel_count = pixels.shape
    joined = plain_join(
        pixels, patch_mask, group_map, embed_weight, mask_token, chan_embed, agg_weight, query_key, group_bias, norm_gain
    )
    section = lax.all_gather(joined, "chan", axis=0, tiled=True)
    flat_heads = head_weight.reshape(-1, own_channels * pixel_count)
    decoded = jnp.dot(section, flat_heads, preferred_element_type=F32) + head_bias.reshape(1, -1)
    return decoded.astype(BF16).reshape(section.shape[0], own_channels, pixel_count)


def pack_kernel(rows, pixels_ref, mask_ref, weight_ref, out_ref):
    peers, pair_rows, width = pixels_ref.shape
    own, locations = mask_ref.shape
    per = locations // peers
    spread = (iota((own, pair_rows), 1) % own == iota((own, pair_rows), 0)).astype(BF16)
    by_location = dot(mask_ref[...].astype(F32).astype(BF16), spread, 0, 0)
    by_location = by_location.reshape(peers, per, pair_rows)
    keep = iota((1, per, pair_rows), 2) // own == iota((1, per, pair_rows), 1)
    hidden = jnp.sum(jnp.where(keep, by_location, 0.0), axis=1)
    visible = 1.0 - hidden
    before = (iota((pair_rows, pair_rows), 0) < iota((pair_rows, pair_rows), 1)).astype(BF16)
    rank = dot(visible.astype(BF16), before)
    place = jnp.where(visible > 0.5, rank, -1.0)
    limit = float(rows - 2)
    over = jnp.max(place, keepdims=True) >= limit
    marked = hidden + jnp.where(over, 2.0, 0.0)
    weight = weight_ref[...]
    high = weight.astype(BF16)
    middle = (weight - high.astype(F32)).astype(BF16)
    low = (weight - high.astype(F32) - middle.astype(F32)).astype(BF16)
    lane = iota((own, width), 1)
    line = iota((own, width), 0)
    weight_row = jnp.zeros((1, width), F32)
    for part, value in enumerate((high, middle, low)):
        weight_row += dot(value, (lane == line + part * own).astype(BF16))
    index = iota((rows, pair_rows), 0).astype(F32)
    for peer in range(peers):
        chosen = (place[peer : peer + 1, :] == index).astype(BF16)
        packed = dot(chosen, pixels_ref[peer])
        line = iota((rows, width), 0)
        mask_row = jnp.pad(marked[peer : peer + 1, :], ((0, 0), (0, width - pair_rows)))
        packed = jnp.where(line == rows - 2, weight_row, packed)
        packed = jnp.where(line == rows - 1, mask_row, packed)
        out_ref[peer] = packed.astype(BF16)


def join_kernel(
    sizes,
    place_ref,
    packed_ref,
    *refs,
):
    sources, own, per, heads, chunk = sizes
    section_refs = refs[: sizes_sections(refs)]
    rest = refs[len(section_refs) :]
    (chan_ref, other_ref, token_ref, query_ref, group_ref, bias_ref, gain_ref, out_ref) = rest[:8]
    (embed, offset, table, choice, where, value, score) = rest[8:]
    _, rows, width = packed_ref.shape
    total = sources * rows
    features = embed.shape[1]
    channels = sources * own
    pair_rows = per * own
    depth = features // heads
    chunks = total // chunk

    me_loc = place_ref[0]
    me = place_ref[1]
    sections = len(section_refs)
    part = features // sections
    for step, section in enumerate(section_refs):
        at = lax.rem(me_loc + step, sections) * part
        embed[:, pl.ds(pl.multiple_of(at, part), part)] = section[...]
    half = sources // 2
    for step in range(half):
        for ref, flip in ((chan_ref, 0), (other_ref, 1)):
            source = jnp.bitwise_xor(me, 2 * step + flip)
            offset[pl.ds(pl.multiple_of(source * own, own), own), :] = ref[step * own : (step + 1) * own, :]

    last = [packed_ref[s, rows - 16 :, :].astype(F32) for s in range(sources)]
    marked = jnp.concatenate([tail[15:16, :] for tail in last], axis=0)[:, :pair_rows]
    weight_rows = jnp.concatenate([tail[14:15, :] for tail in last], axis=0)
    hidden = jnp.where(marked >= 2.0, marked - 2.0, marked)
    visible = 1.0 - hidden
    before = (iota((pair_rows, pair_rows), 0) < iota((pair_rows, pair_rows), 1)).astype(BF16)
    rank = dot(visible.astype(BF16), before)
    place = jnp.where(visible > 0.5, rank, -1.0)
    index = iota((rows, pair_rows), 0).astype(F32)
    of_row = iota((pair_rows, LANES), 0) // own
    to_location = (of_row == iota((pair_rows, LANES), 1)).astype(BF16)
    channel_of_row = iota((pair_rows, channels), 0) % own
    for s in range(sources):
        chosen = (place[s : s + 1, :] == index).astype(BF16)
        to_channel = (channel_of_row + s * own == iota((pair_rows, channels), 1)).astype(BF16)
        choice[s * rows : (s + 1) * rows, :] = dot(chosen, to_channel).astype(BF16)
        where[s * rows : (s + 1) * rows, :] = dot(chosen, to_location).astype(BF16)
    lane = iota((width, channels), 0)
    spread = ((lane % own == iota((width, channels), 1) % own) & (lane < 3 * own)).astype(BF16)
    each = dot(weight_rows.astype(BF16), spread)
    mine = iota((sources, channels), 1) // own == iota((sources, channels), 0)
    weight = jnp.sum(jnp.where(mine, each, 0.0), axis=0, keepdims=True)

    block = 256
    for at in range(0, features, block):
        cols = slice(at, at + block)
        table[:, cols] = gelu(token_ref[:, cols].astype(F32) + offset[:, cols].astype(F32)).astype(BF16)
    table_score = dot(query_ref[...], table[...], 1, 1)

    eye = (iota((per, LANES), 0) == iota((per, LANES), 1)).astype(BF16)
    tile = 128
    counts = jnp.zeros((per, channels), F32)
    spread_score = jnp.zeros((heads * per, channels), F32)
    for c in range(chunks):
        base = c * chunk
        for at in range(0, features, block):
            cols = slice(at, at + block)
            for top in range(base, base + chunk, tile):
                line = slice(top, top + tile)
                pixel = packed_ref[...].reshape(total, width)[line, :]
                pre = dot(pixel, embed[:, cols]) + dot(choice[line, :], offset[:, cols])
                value[line, cols] = gelu(pre).astype(BF16)
        line = slice(base, base + chunk)
        score[c] = dot(query_ref[...], value[line, :], 1, 1)
        at_location = dot(eye, where[line, :], 1, 1)
        counts += dot(at_location.astype(BF16), choice[line, :])
        by_row = [score[c, h : h + 1, :] * at_location for h in range(heads)]
        for piece in halves(jnp.concatenate(by_row, axis=0)):
            spread_score += dot(piece, choice[line, :])

    hidden_at = 1.0 - counts
    by_row = [hidden_at * table_score[h : h + 1, :] for h in range(heads)]
    full = (spread_score + jnp.concatenate(by_row, axis=0)) * weight
    groups = bias_ref.shape[1]
    to_group = (iota((groups, channels), 0) == group_ref[...]).astype(BF16)
    scores = sum(dot(piece, to_group, 1, 1) for piece in halves(full))
    scores += jnp.concatenate([jnp.broadcast_to(bias_ref[h : h + 1, :], (per, groups)) for h in range(heads)], axis=0)
    scores = jnp.exp(scores - jnp.max(scores, axis=-1, keepdims=True))
    attention = scores / jnp.sum(scores, axis=-1, keepdims=True)
    each = sum(dot(piece, to_group) for piece in halves(attention)) * weight

    of_table = halves(each * jnp.concatenate([hidden_at] * heads, axis=0))
    each = halves(each)
    pooled = [jnp.zeros((2 * per, depth), F32)] * heads

    def stack(pieces, h):
        return jnp.concatenate([piece[h * per : (h + 1) * per, :] for piece in pieces], axis=0)

    for h in range(heads):
        pooled[h] += dot(stack(of_table, h), table[:, h * depth : (h + 1) * depth])
    for c in range(chunks):
        line = slice(c * chunk, (c + 1) * chunk)
        at_location = dot(eye, where[line, :], 1, 1)
        spread_each = sum(dot(piece, choice[line, :], 1, 1) for piece in each)
        pieces = halves(spread_each * jnp.concatenate([at_location] * heads, axis=0))
        for h in range(heads):
            pooled[h] += dot(stack(pieces, h), value[line, h * depth : (h + 1) * depth])
    pooled = [both[:per] + both[per:] for both in pooled]
    square = sum(jnp.sum(rows_of * rows_of, axis=-1, keepdims=True) for rows_of in pooled)
    scale = lax.rsqrt(square * (1.0 / features) + 1e-06)
    for h in range(heads):
        cols = slice(h * depth, (h + 1) * depth)
        out_ref[:, cols] = (pooled[h] * scale * gain_ref[:, cols]).astype(BF16)


def sizes_sections(refs):
    return len(refs) - 15


def decode_kernel(place_ref, near_ref, far_ref, head_ref, bias_ref, out_ref, heads, line, arrived):
    own = bias_ref.shape[0]
    half = near_ref.shape[0]
    per = out_ref.shape[1]
    me = place_ref[1]
    copies = [pltpu.make_async_copy(head_ref.at[c], heads.at[c], arrived.at[c]) for c in range(own)]
    for copy in copies:
        copy.start()
    for c in range(own):
        copies[c].wait()
        for flip, ref in ((0, near_ref), (1, far_ref)):
            decoded = dot(ref[...], heads[c]) + bias_ref[c : c + 1, :]
            for step in range(half // per):
                owner = jnp.bitwise_xor(me, 2 * step + flip)
                line[owner, :, c, :] = decoded[step * per : (step + 1) * per, :]
    for owner in range(2 * half // per):
        out_ref[owner] = line[owner].astype(BF16)


def flipped(value, axis, count, flip):
    return lax.ppermute(value, axis, [(i, i ^ flip) for i in range(count)])


def spread_rows(value, axis, count):
    near = [value] + [flipped(value, axis, count, 2 * k) for k in range(1, count // 2)]
    near = jnp.concatenate(near, axis=0)
    return near, flipped(near, axis, count, 1)


def whole(value):
    return jax.ShapeDtypeStruct(value[0], value[1])


def shards(
    peers,
    blocks,
    pixels,
    patch_mask,
    group_map,
    embed_weight,
    mask_token,
    chan_embed,
    agg_weight,
    query_key,
    group_bias,
    norm_gain,
    head_weight,
    head_bias,
):
    locations, own, pixel_count = pixels.shape
    channels = group_map.shape[0]
    heads, features = query_key.shape
    per = locations // peers
    pair_rows = per * own
    rows = -(-pair_rows * 3 // 8 // 16) * 16
    total = peers * rows
    fits = (
        peers & (peers - 1) == 0
        and own % 16 == 0
        and per % 16 == 0
        and pair_rows <= pixel_count
        and 3 * own <= pixel_count
        and total % 512 == 0
    )
    if not fits:
        return plain_shards(
            pixels,
            patch_mask,
            group_map,
            embed_weight,
            mask_token,
            chan_embed,
            agg_weight,
            query_key,
            group_bias,
            norm_gain,
            head_weight,
            head_bias,
        )
    vmem = pltpu.CompilerParams(vmem_limit_bytes=48 << 20)
    place = jnp.stack([lax.axis_index("loc"), lax.axis_index("chan")]).astype(jnp.int32)

    packed = pl.pallas_call(
        functools.partial(pack_kernel, rows),
        out_shape=jax.ShapeDtypeStruct((peers, rows, pixel_count), BF16),
        in_specs=[VMEM] * 3,
        out_specs=VMEM,
        compiler_params=vmem,
        name="pack",
    )(pixels.reshape(peers, pair_rows, pixel_count), patch_mask.T, agg_weight.reshape(1, own))
    sections = [embed_weight]
    for step in range(1, blocks):
        hop = [(i, (i - step) % blocks) for i in range(blocks)]
        sections.append(lax.ppermute(embed_weight, "loc", hop))
    near, far = spread_rows(chan_embed, "chan", peers)
    packed = lax.all_to_all(packed, "chan", split_axis=0, concat_axis=0, tiled=True)

    over = jnp.max((packed[:, rows - 1, :LANES].astype(F32) >= 2.0).astype(jnp.int32))
    over = jnp.broadcast_to(over, (8, LANES))
    most = over
    for step in range(1, blocks):
        hop = [(i, (i - step) % blocks) for i in range(blocks)]
        most = jnp.maximum(most, lax.ppermute(over, "loc", hop))

    chunk = 512
    joined = pl.pallas_call(
        functools.partial(join_kernel, (peers, own, per, heads, chunk)),
        out_shape=jax.ShapeDtypeStruct((per, features), BF16),
        in_specs=[pl.BlockSpec(memory_space=pltpu.SMEM)] + [VMEM] * (8 + blocks),
        out_specs=VMEM,
        scratch_shapes=[
            pltpu.VMEM((pixel_count, features), BF16),
            pltpu.VMEM((channels, features), BF16),
            pltpu.VMEM((channels, features), BF16),
            pltpu.VMEM((total, channels), BF16),
            pltpu.VMEM((total, LANES), BF16),
            pltpu.VMEM((total, features), BF16),
            pltpu.VMEM((total // chunk, heads, chunk), F32),
        ],
        compiler_params=vmem,
        name="join",
    )(
        place,
        packed,
        *sections,
        near,
        far,
        mask_token.reshape(1, features),
        query_key,
        group_map.reshape(1, channels),
        group_bias,
        norm_gain.reshape(1, features),
    )
    joined = lax.cond(
        most[0, 0] > 0,
        lambda: plain_join(
            pixels,
            patch_mask,
            group_map,
            embed_weight,
            mask_token,
            chan_embed,
            agg_weight,
            query_key,
            group_bias,
            norm_gain,
        ),
        lambda: joined,
    )
    near, far = spread_rows(joined, "chan", peers)
    by_channel = jnp.transpose(head_weight, (1, 0, 2))
    rebuilt = pl.pallas_call(
        decode_kernel,
        out_shape=jax.ShapeDtypeStruct((peers, per, own, pixel_count), BF16),
        in_specs=[pl.BlockSpec(memory_space=pltpu.SMEM), VMEM, VMEM, ANY, VMEM],
        out_specs=VMEM,
        scratch_shapes=[
            pltpu.VMEM((own, features, pixel_count), BF16),
            pltpu.VMEM((peers, per, own, pixel_count), F32),
            pltpu.SemaphoreType.DMA((own,)),
        ],
        compiler_params=vmem,
        name="decode",
    )(place, near, far, by_channel, head_bias)
    return rebuilt.reshape(locations, own, pixel_count)


def solution(mesh):
    return jax.shard_map(
        functools.partial(shards, mesh.shape["chan"], mesh.shape["loc"]),
        mesh=mesh,
        in_specs=(
            P("loc", "chan", None),
            P("loc", "chan"),
            P(),
            P(None, "loc"),
            P(),
            P("chan", None),
            P("chan"),
            P(),
            P(),
            P(),
            P(None, "chan", None),
            P("chan", None),
        ),
        out_specs=P("loc", "chan", None),
        check_vma=False,
    )
```

profile of v0, /device:TPU:0, one launch (start us, length us, event | category | flops | bytes accessed | tf_op | source)
XLA Modules:
  0.0 119.5 jit_solution(4689809339242360370)
XLA Ops:
  6.5 3.0 %collective-permute-start.2 = (bf16[16,2048]{1,0:T(8,128)(2,1)}, bf16[16,2048]{1,0:T(8,128)(2,1)S(1)}, u32[]{:S(2)}, u32[]{:S(2)}) collective-permute-start(bf16[16,2048]{1,0:T(8,128)(2,1)} %param.19), channel_id=1, source_target_pairs={{0,4},{2,6},{4,0},{6,2},{8,12},{10,14},{12,8},{14,10},{16,20},{18,... | collective-permute-start | bytes 196616 | tf_op jit(solution)/shard_map/ppermute | solution.py:284
  9.5 1.6 %collective-permute-start.3 = (bf16[16,2048]{1,0:T(8,128)(2,1)}, bf16[16,2048]{1,0:T(8,128)(2,1)S(1)}, u32[]{:S(2)}, u32[]{:S(2)}) collective-permute-start(bf16[16,2048]{1,0:T(8,128)(2,1)} %param.19), channel_id=1, source_target_pairs={{0,8},{2,10},{4,12},{6,14},{8,0},{10,2},{12,4},{14,6},{16,24},{18,... | collective-permute-start | bytes 196616 | tf_op jit(solution)/shard_map/ppermute | solution.py:284
  11.1 3.0 %collective-permute-start.5 = (bf16[16,2048]{1,0:T(8,128)(2,1)}, bf16[16,2048]{1,0:T(8,128)(2,1)S(1)}, u32[]{:S(2)}, u32[]{:S(2)}) collective-permute-start(bf16[16,2048]{1,0:T(8,128)(2,1)} %param.19), channel_id=1, source_target_pairs={{0,16},{2,18},{4,20},{6,22},{8,24},{10,26},{12,28},{14,30},{16,0},... | collective-permute-start | bytes 196616 | tf_op jit(solution)/shard_map/ppermute | solution.py:284
  14.1 1.3 %collective-permute-start.6 = (bf16[16,2048]{1,0:T(8,128)(2,1)}, bf16[16,2048]{1,0:T(8,128)(2,1)S(1)}, u32[]{:S(2)}, u32[]{:S(2)}) collective-permute-start(bf16[16,2048]{1,0:T(8,128)(2,1)} %param.19), channel_id=1, source_target_pairs={{0,20},{2,22},{4,16},{6,18},{8,28},{10,30},{12,24},{14,26},{16,4},... | collective-permute-start | bytes 196616 | tf_op jit(solution)/shard_map/ppermute | solution.py:284
  15.4 3.3 %pack.1 = bf16[16,96,256]{2,1,0:T(8,128)(2,1)} custom-call(bf16[16,256,256]{2,1,0:T(8,128)(2,1)} %bitcast.81, s32[16,256]{1,0:T(8,128)} %bitcast.89, f32[1,16]{1,0:T(1,128)} %bitcast.94), custom_call_target="tpu_custom_call" | custom-call | tf_op jit(solution)/shard_map/pack/pallas_call | solution.py:346
  18.7 5.0 %all-to-all-start.2 = ((bf16[16,96,256]{2,1,0:T(8,128)(2,1)}), bf16[16,96,256]{2,1,0:T(8,128)(2,1)S(1)}, u32[]{:S(2)}, u32[]{:S(2)}) async-start(bf16[16,96,256]{2,1,0:T(8,128)(2,1)} %pack.1), calls=%async_computation.2 | async-start | bytes 1572864 | tf_op jit(solution)/shard_map/all_to_all | solution.py:359
  24.5 3.7 %collective-permute-start.7 = (bf16[16,2048]{1,0:T(8,128)(2,1)}, bf16[16,2048]{1,0:T(8,128)(2,1)S(1)}, u32[]{:S(2)}, u32[]{:S(2)}) collective-permute-start(bf16[16,2048]{1,0:T(8,128)(2,1)} %param.19), channel_id=1, source_target_pairs={{0,24},{2,26},{4,28},{6,30},{8,16},{10,18},{12,20},{14,22},{16,8},... | collective-permute-start | bytes 196616 | tf_op jit(solution)/shard_map/ppermute | solution.py:284
  28.2 1.5 %collective-permute-start.8 = (bf16[16,2048]{1,0:T(8,128)(2,1)}, bf16[16,2048]{1,0:T(8,128)(2,1)S(1)}, u32[]{:S(2)}, u32[]{:S(2)}) collective-permute-start(bf16[16,2048]{1,0:T(8,128)(2,1)} %param.19), channel_id=1, source_target_pairs={{0,28},{2,30},{4,24},{6,26},{8,20},{10,22},{12,16},{14,18},{16,12}... | collective-permute-start | bytes 196616 | tf_op jit(solution)/shard_map/ppermute | solution.py:284
  29.8 1.6 %collective-permute-start.1 = (bf16[256,1024]{1,0:T(8,128)(2,1)}, bf16[256,1024]{1,0:T(8,128)(2,1)S(1)}, u32[]{:S(2)}, u32[]{:S(2)}) collective-permute-start(bf16[256,1024]{1,0:T(8,128)(2,1)} %refs_0_.1), channel_id=1, source_target_pairs={{0,1},{1,0},{2,3},{3,2},{4,5},{5,4},{6,7},{7,6},{8,9},{9,8},{10,11... | collective-permute-start | bytes 1572872 | tf_op jit(solution)/shard_map/ppermute | solution.py:357
  31.4 12.0 %collective-permute-done.7 = bf16[16,2048]{1,0:T(8,128)(2,1)S(1)} collective-permute-done((bf16[16,2048]{1,0:T(8,128)(2,1)}, bf16[16,2048]{1,0:T(8,128)(2,1)S(1)}, u32[]{:S(2)}, u32[]{:S(2)}) %collective-permute-start.7) | collective-permute-done | bytes 65568 | tf_op jit(solution)/shard_map/ppermute | solution.py:284
  43.3 1.8 %collective-permute-done.8 = bf16[16,2048]{1,0:T(8,128)(2,1)S(1)} collective-permute-done((bf16[16,2048]{1,0:T(8,128)(2,1)}, bf16[16,2048]{1,0:T(8,128)(2,1)S(1)}, u32[]{:S(2)}, u32[]{:S(2)}) %collective-permute-start.8) | collective-permute-done | bytes 65568 | tf_op jit(solution)/shard_map/ppermute | solution.py:284
  46.5 1.6 %collective-permute-start = (s32[8,128]{1,0:T(8,128)S(1)}, s32[8,128]{1,0:T(8,128)S(1)}, u32[]{:S(2)}, u32[]{:S(2)}) collective-permute-start(s32[8,128]{1,0:T(8,128)S(1)} %broadcast_in_dim.20), channel_id=1, source_target_pairs={{0,1},{1,0},{2,3},{3,2},{4,5},{5,4},{6,7},{7,6},{8,9},{9,8},{10,11... | collective-permute-start | bytes 12296 | tf_op jit(solution)/shard_map/ppermute | solution.py:366
  48.8 11.8 %join.1 = bf16[16,2048]{1,0:T(8,128)(2,1)} custom-call(s32[2]{0:T(128)S(1)} %pad_add_fusion.1.place_ref, bf16[16,96,256]{2,1,0:T(8,128)(2,1)S(1)} %all-to-all-done.2.packed_ref, bf16[256,1024]{1,0:T(8,128)(2,1)} %refs_0_.1, bf16[256,1024]{1,0:T(8,128)(2,1)S(1)} %collective-permute-done.1.refs_1_, ...), custom_call_target="tpu_custom_call" | custom-call | tf_op jit(solution)/shard_map/join/pallas_call | solution.py:369
  62.7 1.1 collective-permute-start.10
  64.7 6.0 %collective-permute-start.11 = (bf16[16,2048]{1,0:T(8,128)(2,1)}, bf16[16,2048]{1,0:T(8,128)(2,1)S(1)}, u32[]{:S(2)}, u32[]{:S(2)}) collective-permute-start(bf16[16,2048]{1,0:T(8,128)(2,1)} %get-tuple-element.43), channel_id=1, source_target_pairs={{0,8},{2,10},{4,12},{6,14},{8,0},{10,2},{12,4},{14,6},{16,24},{18,... | collective-permute-start | bytes 196616 | tf_op jit(solution)/shard_map/ppermute | solution.py:284
  70.7 0.9 collective-permute-start.12
  71.6 2.0 %collective-permute-start.13 = (bf16[16,2048]{1,0:T(8,128)(2,1)}, bf16[16,2048]{1,0:T(8,128)(2,1)S(1)}, u32[]{:S(2)}, u32[]{:S(2)}) collective-permute-start(bf16[16,2048]{1,0:T(8,128)(2,1)} %get-tuple-element.43), channel_id=1, source_target_pairs={{0,16},{2,18},{4,20},{6,22},{8,24},{10,26},{12,28},{14,30},{16,0},... | collective-permute-start | bytes 196616 | tf_op jit(solution)/shard_map/ppermute | solution.py:284
  73.6 0.9 collective-permute-start.14
  74.6 1.5 %collective-permute-start.15 = (bf16[16,2048]{1,0:T(8,128)(2,1)}, bf16[16,2048]{1,0:T(8,128)(2,1)S(1)}, u32[]{:S(2)}, u32[]{:S(2)}) collective-permute-start(bf16[16,2048]{1,0:T(8,128)(2,1)} %get-tuple-element.43), channel_id=1, source_target_pairs={{0,24},{2,26},{4,28},{6,30},{8,16},{10,18},{12,20},{14,22},{16,8},... | collective-permute-start | bytes 196616 | tf_op jit(solution)/shard_map/ppermute | solution.py:284
  76.0 3.3 %collective-permute-start.16 = (bf16[16,2048]{1,0:T(8,128)(2,1)}, bf16[16,2048]{1,0:T(8,128)(2,1)S(1)}, u32[]{:S(2)}, u32[]{:S(2)}) collective-permute-start(bf16[16,2048]{1,0:T(8,128)(2,1)} %get-tuple-element.43), channel_id=1, source_target_pairs={{0,28},{2,30},{4,24},{6,26},{8,20},{10,22},{12,16},{14,18},{16,12}... | collective-permute-start | bytes 196616 | tf_op jit(solution)/shard_map/ppermute | solution.py:284
  79.4 3.1 %collective-permute-done.13 = bf16[16,2048]{1,0:T(8,128)(2,1)S(1)} collective-permute-done((bf16[16,2048]{1,0:T(8,128)(2,1)}, bf16[16,2048]{1,0:T(8,128)(2,1)S(1)}, u32[]{:S(2)}, u32[]{:S(2)}) %collective-permute-start.13) | collective-permute-done | bytes 65568 | tf_op jit(solution)/shard_map/ppermute | solution.py:284
  82.5 1.8 %collective-permute-done.14 = bf16[16,2048]{1,0:T(8,128)(2,1)S(1)} collective-permute-done((bf16[16,2048]{1,0:T(8,128)(2,1)}, bf16[16,2048]{1,0:T(8,128)(2,1)S(1)}, u32[]{:S(2)}, u32[]{:S(2)}) %collective-permute-start.14) | collective-permute-done | bytes 65568 | tf_op jit(solution)/shard_map/ppermute | solution.py:284
  84.4 15.7 %copy.70 = bf16[2048,16,256]{2,0,1:T(8,128)(2,1)} copy(bf16[2048,16,256]{2,1,0:T(8,128)(2,1)} %param.24) | data formatting | bytes 33554432 | tf_op args[10]
  100.1 12.6 %decode.1 = bf16[16,16,16,256]{3,2,1,0:T(8,128)(2,1)} custom-call(s32[2]{0:T(128)S(1)} %copy-done.2, bf16[128,2048]{1,0:T(8,128)(2,1)S(1)} %constant_dynamic-update-slice_fusion.8.near_ref, bf16[128,2048]{1,0:T(8,128)(2,1)S(1)} %collective-permute-done.17.far_ref, bf16[16,2048,256]{2,1,0:T(8,128)(2,1)} %bitcast.79, f32[16,256]{1,0:T(8,128)S(1)} %copy-done), custom_call_target="tpu_custom_call" | custom-call | tf_op jit(solution)/shard_map/decode/pallas_call | solution.py:415
  (47 shorter events, 5.4 us)
Async XLA Ops:
  6.5 18.0 %collective-permute-start.2 = (bf16[16,2048]{1,0:T(8,128)(2,1)}, bf16[16,2048]{1,0:T(8,128)(2,1)S(1)}, u32[]{:S(2)}, u32[]{:S(2)}) collective-permute-start(bf16[16,2048]{1,0:T(8,128)(2,1)} %param.19), channel_id=1, source_target_pairs={{0,4},{2,6},{4,0},{6,2},{8,12},{10,14},{12,8},{14,10},{16,20},{18,... | collective-permute-start | bytes 196616 | tf_op jit(solution)/shard_map/ppermute | solution.py:284
  9.5 18.7 %collective-permute-start.3 = (bf16[16,2048]{1,0:T(8,128)(2,1)}, bf16[16,2048]{1,0:T(8,128)(2,1)S(1)}, u32[]{:S(2)}, u32[]{:S(2)}) collective-permute-start(bf16[16,2048]{1,0:T(8,128)(2,1)} %param.19), channel_id=1, source_target_pairs={{0,8},{2,10},{4,12},{6,14},{8,0},{10,2},{12,4},{14,6},{16,24},{18,... | collective-permute-start | bytes 196616 | tf_op jit(solution)/shard_map/ppermute | solution.py:284
  11.1 18.7 %collective-permute-start.4 = (bf16[16,2048]{1,0:T(8,128)(2,1)}, bf16[16,2048]{1,0:T(8,128)(2,1)S(1)}, u32[]{:S(2)}, u32[]{:S(2)}) collective-permute-start(bf16[16,2048]{1,0:T(8,128)(2,1)} %param.19), channel_id=1, source_target_pairs={{0,12},{2,14},{4,8},{6,10},{8,4},{10,6},{12,0},{14,2},{16,28},{18,... | collective-permute-start | bytes 196616 | tf_op jit(solution)/shard_map/ppermute | solution.py:284
  11.1 20.3 %collective-permute-start.5 = (bf16[16,2048]{1,0:T(8,128)(2,1)}, bf16[16,2048]{1,0:T(8,128)(2,1)S(1)}, u32[]{:S(2)}, u32[]{:S(2)}) collective-permute-start(bf16[16,2048]{1,0:T(8,128)(2,1)} %param.19), channel_id=1, source_target_pairs={{0,16},{2,18},{4,20},{6,22},{8,24},{10,26},{12,28},{14,30},{16,0},... | collective-permute-start | bytes 196616 | tf_op jit(solution)/shard_map/ppermute | solution.py:284
  14.1 17.3 %collective-permute-start.6 = (bf16[16,2048]{1,0:T(8,128)(2,1)}, bf16[16,2048]{1,0:T(8,128)(2,1)S(1)}, u32[]{:S(2)}, u32[]{:S(2)}) collective-permute-start(bf16[16,2048]{1,0:T(8,128)(2,1)} %param.19), channel_id=1, source_target_pairs={{0,20},{2,22},{4,16},{6,18},{8,28},{10,30},{12,24},{14,26},{16,4},... | collective-permute-start | bytes 196616 | tf_op jit(solution)/shard_map/ppermute | solution.py:284
  18.7 26.5 %all-to-all-start.2 = ((bf16[16,96,256]{2,1,0:T(8,128)(2,1)}), bf16[16,96,256]{2,1,0:T(8,128)(2,1)S(1)}, u32[]{:S(2)}, u32[]{:S(2)}) async-start(bf16[16,96,256]{2,1,0:T(8,128)(2,1)} %pack.1), calls=%async_computation.2 | async-start | bytes 1572864 | tf_op jit(solution)/shard_map/all_to_all | solution.py:359
  24.5 18.8 %collective-permute-start.7 = (bf16[16,2048]{1,0:T(8,128)(2,1)}, bf16[16,2048]{1,0:T(8,128)(2,1)S(1)}, u32[]{:S(2)}, u32[]{:S(2)}) collective-permute-start(bf16[16,2048]{1,0:T(8,128)(2,1)} %param.19), channel_id=1, source_target_pairs={{0,24},{2,26},{4,28},{6,30},{8,16},{10,18},{12,20},{14,22},{16,8},... | collective-permute-start | bytes 196616 | tf_op jit(solution)/shard_map/ppermute | solution.py:284
  28.2 16.9 %collective-permute-start.8 = (bf16[16,2048]{1,0:T(8,128)(2,1)}, bf16[16,2048]{1,0:T(8,128)(2,1)S(1)}, u32[]{:S(2)}, u32[]{:S(2)}) collective-permute-start(bf16[16,2048]{1,0:T(8,128)(2,1)} %param.19), channel_id=1, source_target_pairs={{0,28},{2,30},{4,24},{6,26},{8,20},{10,22},{12,16},{14,18},{16,12}... | collective-permute-start | bytes 196616 | tf_op jit(solution)/shard_map/ppermute | solution.py:284
  29.8 19.1 %collective-permute-start.1 = (bf16[256,1024]{1,0:T(8,128)(2,1)}, bf16[256,1024]{1,0:T(8,128)(2,1)S(1)}, u32[]{:S(2)}, u32[]{:S(2)}) collective-permute-start(bf16[256,1024]{1,0:T(8,128)(2,1)} %refs_0_.1), channel_id=1, source_target_pairs={{0,1},{1,0},{2,3},{3,2},{4,5},{5,4},{6,7},{7,6},{8,9},{9,8},{10,11... | collective-permute-start | bytes 1572872 | tf_op jit(solution)/shard_map/ppermute | solution.py:357
  45.2 3.7 %collective-permute-start.9 = (bf16[128,2048]{1,0:T(8,128)(2,1)S(1)}, bf16[128,2048]{1,0:T(8,128)(2,1)S(1)}, u32[]{:S(2)}, u32[]{:S(2)}) collective-permute-start(bf16[128,2048]{1,0:T(8,128)(2,1)S(1)} %constant_dynamic-update-slice_fusion.refs_2_), channel_id=1, source_target_pairs={{0,2},{2,0},{4,6},{6,4},{8,10},{10,8},{12,14},{14,12},{16,18},{18,... | collective-permute-start | bytes 1572872 | tf_op jit(solution)/shard_map/ppermute | solution.py:284
  46.5 14.2 %collective-permute-start = (s32[8,128]{1,0:T(8,128)S(1)}, s32[8,128]{1,0:T(8,128)S(1)}, u32[]{:S(2)}, u32[]{:S(2)}) collective-permute-start(s32[8,128]{1,0:T(8,128)S(1)} %broadcast_in_dim.20), channel_id=1, source_target_pairs={{0,1},{1,0},{2,3},{3,2},{4,5},{5,4},{6,7},{7,6},{8,9},{9,8},{10,11... | collective-permute-start | bytes 12296 | tf_op jit(solution)/shard_map/ppermute | solution.py:366
  48.1 12.5 %copy-start.1 = (s32[2]{0:T(128)}, s32[2]{0:T(128)S(1)}, u32[]{:S(2)}) copy-start(s32[2]{0:T(128)S(1)} %pad_add_fusion.1.place_ref) | copy-start | bytes 28
  62.7 11.8 %collective-permute-start.10 = (bf16[16,2048]{1,0:T(8,128)(2,1)}, bf16[16,2048]{1,0:T(8,128)(2,1)S(1)}, u32[]{:S(2)}, u32[]{:S(2)}) collective-permute-start(bf16[16,2048]{1,0:T(8,128)(2,1)} %get-tuple-element.43), channel_id=1, source_target_pairs={{0,4},{2,6},{4,0},{6,2},{8,12},{10,14},{12,8},{14,10},{16,20},{18,... | collective-permute-start | bytes 196616 | tf_op jit(solution)/shard_map/ppermute | solution.py:284
  64.7 11.3 %collective-permute-start.11 = (bf16[16,2048]{1,0:T(8,128)(2,1)}, bf16[16,2048]{1,0:T(8,128)(2,1)S(1)}, u32[]{:S(2)}, u32[]{:S(2)}) collective-permute-start(bf16[16,2048]{1,0:T(8,128)(2,1)} %get-tuple-element.43), channel_id=1, source_target_pairs={{0,8},{2,10},{4,12},{6,14},{8,0},{10,2},{12,4},{14,6},{16,24},{18,... | collective-permute-start | bytes 196616 | tf_op jit(solution)/shard_map/ppermute | solution.py:284
  70.7 8.6 %collective-permute-start.12 = (bf16[16,2048]{1,0:T(8,128)(2,1)}, bf16[16,2048]{1,0:T(8,128)(2,1)S(1)}, u32[]{:S(2)}, u32[]{:S(2)}) collective-permute-start(bf16[16,2048]{1,0:T(8,128)(2,1)} %get-tuple-element.43), channel_id=1, source_target_pairs={{0,12},{2,14},{4,8},{6,10},{8,4},{10,6},{12,0},{14,2},{16,28},{18,... | collective-permute-start | bytes 196616 | tf_op jit(solution)/shard_map/ppermute | solution.py:284
  71.6 10.8 %collective-permute-start.13 = (bf16[16,2048]{1,0:T(8,128)(2,1)}, bf16[16,2048]{1,0:T(8,128)(2,1)S(1)}, u32[]{:S(2)}, u32[]{:S(2)}) collective-permute-start(bf16[16,2048]{1,0:T(8,128)(2,1)} %get-tuple-element.43), channel_id=1, source_target_pairs={{0,16},{2,18},{4,20},{6,22},{8,24},{10,26},{12,28},{14,30},{16,0},... | collective-permute-start | bytes 196616 | tf_op jit(solution)/shard_map/ppermute | solution.py:284
  73.6 10.6 %collective-permute-start.14 = (bf16[16,2048]{1,0:T(8,128)(2,1)}, bf16[16,2048]{1,0:T(8,128)(2,1)S(1)}, u32[]{:S(2)}, u32[]{:S(2)}) collective-permute-start(bf16[16,2048]{1,0:T(8,128)(2,1)} %get-tuple-element.43), channel_id=1, source_target_pairs={{0,20},{2,22},{4,16},{6,18},{8,28},{10,30},{12,24},{14,26},{16,4},... | collective-permute-start | bytes 196616 | tf_op jit(solution)/shard_map/ppermute | solution.py:284
  74.6 9.7 %collective-permute-start.15 = (bf16[16,2048]{1,0:T(8,128)(2,1)}, bf16[16,2048]{1,0:T(8,128)(2,1)S(1)}, u32[]{:S(2)}, u32[]{:S(2)}) collective-permute-start(bf16[16,2048]{1,0:T(8,128)(2,1)} %get-tuple-element.43), channel_id=1, source_target_pairs={{0,24},{2,26},{4,28},{6,30},{8,16},{10,18},{12,20},{14,22},{16,8},... | collective-permute-start | bytes 196616 | tf_op jit(solution)/shard_map/ppermute | solution.py:284
  76.0 8.2 %collective-permute-start.16 = (bf16[16,2048]{1,0:T(8,128)(2,1)}, bf16[16,2048]{1,0:T(8,128)(2,1)S(1)}, u32[]{:S(2)}, u32[]{:S(2)}) collective-permute-start(bf16[16,2048]{1,0:T(8,128)(2,1)} %get-tuple-element.43), channel_id=1, source_target_pairs={{0,28},{2,30},{4,24},{6,26},{8,20},{10,22},{12,16},{14,18},{16,12}... | collective-permute-start | bytes 196616 | tf_op jit(solution)/shard_map/ppermute | solution.py:284
  84.3 15.8 %copy-start = (f32[16,256]{1,0:T(8,128)S(1)}, f32[16,256]{1,0:T(8,128)}, u32[]{:S(2)}) copy-start(f32[16,256]{1,0:T(8,128)} %bias_ref.1) | copy-start | bytes 49156
  84.3 15.8 %copy-start.2 = (s32[2]{0:T(128)S(1)}, s32[2]{0:T(128)}, u32[]{:S(2)}) copy-start(s32[2]{0:T(128)} %copy-done.1) | copy-start | bytes 28
  84.3 15.8 %collective-permute-start.17 = (bf16[128,2048]{1,0:T(8,128)(2,1)S(1)}, bf16[128,2048]{1,0:T(8,128)(2,1)S(1)}, u32[]{:S(2)}, u32[]{:S(2)}) collective-permute-start(bf16[128,2048]{1,0:T(8,128)(2,1)S(1)} %constant_dynamic-update-slice_fusion.8.near_ref), channel_id=1, source_target_pairs={{0,2},{2,0},{4,6},{6,4},{8,10},{10,8},{12,14},{14,12},{16,18},{18,... | collective-permute-start | bytes 1572872 | tf_op jit(solution)/shard_map/ppermute | solution.py:284
where the time goes:
time: 121 us; the launch traced here: 119 us
  starting transfers between devices  38 us (31%)
  Pallas kernels  27.7 us (23%)
  local copies, waits for them, and re-layouts  19.3 us (16%)
  waiting for transfers between devices  18.7 us (15%)
  between operations  14.2 us (12%)
  other arithmetic  1.37 us (1%)
    ppermute x16, starting transfers between devices, flipped(): return lax.ppermute(value, axis, [(i, i ^ flip) for i in range(count)])  29.9 us
    ppermute x16, waiting for transfers between devices, flipped(): return lax.ppermute(value, axis, [(i, i ^ flip) for i in range(count)])  18.7 us
    unnamed x21, local copies, waits for them, and re-layouts  17.5 us
    pallas_call x1, Pallas kernels, shards(): pl.pallas_call(decode_kernel, out_shape=jax.ShapeDtypeStruct((peers, per,...  12.6 us
    pallas_call x1, Pallas kernels, shards(): pl.pallas_call(functools.partial(join_kernel, (peers, own, per, heads, ch...  11.8 us
    all_to_all x1, starting transfers between devices, shards(): lax.all_to_all(packed, 'chan', split_axis=0, concat_axis=0, tiled=True)  4.98 us
    pallas_call x1, Pallas kernels, shards(): pl.pallas_call(functools.partial(pack_kernel, rows), out_shape=jax.ShapeD...  3.3 us
  transfers between devices with their start and end apart: 19, of which 4 were waited for; matrix products, arithmetic and copies ran while one was open for 16% of the time, Pallas kernels for 13%

commit v1 on v0

--- a/solution.py
+++ b/solution.py
@@ -11,6 +11,7 @@
 BUNDLE = 4
 LANES = 128
 VMEM = pl.BlockSpec(memory_space=pltpu.VMEM)
+SMEM = pl.BlockSpec(memory_space=pltpu.SMEM)
 ANY = pl.BlockSpec(memory_space=pl.ANY)
 F32, BF16 = jnp.float32, jnp.bfloat16
 
@@ -56,6 +57,14 @@
     return (pooled * inverse_rms * norm_gain[None]).astype(BF16)
 
 
+def gathered(value, axis, dim):
+    count = lax.axis_size(axis)
+    copies = jnp.broadcast_to(value[None], (count,) + value.shape)
+    parts = lax.all_to_all(copies, axis, split_axis=0, concat_axis=0, tiled=True)
+    parts = jnp.moveaxis(parts, 0, dim)
+    return parts.reshape(value.shape[:dim] + (-1,) + value.shape[dim + 1 :])
+
+
 def plain_join(
     pixels, patch_mask, group_map, embed_weight, mask_token, chan_embed, agg_weight, query_key, group_bias, norm_gain
 ):
@@ -63,9 +72,9 @@
     choose, to_group = slot_tables(group_map)
     source_pixels = lax.all_to_all(pixels, "chan", split_axis=0, concat_axis=1, tiled=True)
     source_mask = lax.all_to_all(patch_mask, "chan", split_axis=0, concat_axis=1, tiled=True)
-    offsets = lax.all_gather(chan_embed, "chan", axis=0, tiled=True).astype(F32)
-    weights = lax.all_gather(agg_weight, "chan", axis=0, tiled=True)
-    section = lax.all_gather(embed_weight, "loc", axis=1, tiled=True)
+    offsets = gathered(chan_embed, "chan", 0).astype(F32)
+    weights = gathered(agg_weight, "chan", 0)
+    section = gathered(embed_weight, "loc", 1)
     rows, channels, _ = source_pixels.shape
     features = section.shape[1]
     projected = jnp.dot(source_pixels.reshape(rows * channels, pixel_count), section, preferred_element_type=F32)
@@ -98,7 +107,7 @@
     joined = plain_join(
         pixels, patch_mask, group_map, embed_weight, mask_token, chan_embed, agg_weight, query_key, group_bias, norm_gain
     )
-    section = lax.all_gather(joined, "chan", axis=0, tiled=True)
+    section = gathered(joined, "chan", 0)
     flat_heads = head_weight.reshape(-1, own_channels * pixel_count)
     decoded = jnp.dot(section, flat_heads, preferred_element_type=F32) + head_bias.reshape(1, -1)
     return decoded.astype(BF16).reshape(section.shape[0], own_channels, pixel_count)
@@ -140,6 +149,23 @@
         out_ref[peer] = packed.astype(BF16)
 
 
+def by_channel_kernel(start, head_ref, out_ref, blocks, arrived):
+    _, depth, own, width = blocks.shape
+    steps = out_ref.shape[1] // depth
+
+    def fetch(step):
+        slot = step % 2
+        rows = pl.ds(start + step * depth, depth)
+        return pltpu.make_async_copy(head_ref.at[rows], blocks.at[slot], arrived.at[slot])
+
+    fetch(0).start()
+    for step in range(steps):
+        if step + 1 < steps:
+            fetch(step + 1).start()
+        fetch(step).wait()
+        out_ref[:, step * depth : (step + 1) * depth, :] = jnp.swapaxes(blocks[step % 2], 0, 1)
+
+
 def join_kernel(
     sizes,
     place_ref,
@@ -149,8 +175,8 @@
     sources, own, per, heads, chunk = sizes
     section_refs = refs[: sizes_sections(refs)]
     rest = refs[len(section_refs) :]
-    (chan_ref, other_ref, token_ref, query_ref, group_ref, bias_ref, gain_ref, out_ref) = rest[:8]
-    (embed, offset, table, choice, where, value, score) = rest[8:]
+    (chan_ref, other_ref, token_ref, query_ref, group_ref, bias_ref, gain_ref, out_ref, over_ref) = rest[:9]
+    (embed, offset, table, choice, where, value, score) = rest[9:]
     _, rows, width = packed_ref.shape
     total = sources * rows
     features = embed.shape[1]
@@ -175,6 +201,8 @@
     last = [packed_ref[s, rows - 16 :, :].astype(F32) for s in range(sources)]
     marked = jnp.concatenate([tail[15:16, :] for tail in last], axis=0)[:, :pair_rows]
     weight_rows = jnp.concatenate([tail[14:15, :] for tail in last], axis=0)
+    over = jnp.max((marked >= 2.0).astype(F32), keepdims=True)
+    over_ref[...] = jnp.broadcast_to(over, over_ref.shape).astype(jnp.int32)
     hidden = jnp.where(marked >= 2.0, marked - 2.0, marked)
     visible = 1.0 - hidden
     before = (iota((pair_rows, pair_rows), 0) < iota((pair_rows, pair_rows), 1)).astype(BF16)
@@ -258,26 +286,27 @@
 
 
 def sizes_sections(refs):
-    return len(refs) - 15
-
-
-def decode_kernel(place_ref, near_ref, far_ref, head_ref, bias_ref, out_ref, heads, line, arrived):
+    return len(refs) - 16
+
+
+def decode_kernel(place_ref, near_ref, far_ref, low_ref, high_ref, bias_ref, *refs):
+    *most, out_ref, over_ref, joined, decoded = refs
     own = bias_ref.shape[0]
+    over_ref[0] = jnp.max(functools.reduce(jnp.maximum, [ref[...] for ref in most]))
     half = near_ref.shape[0]
     per = out_ref.shape[1]
     me = place_ref[1]
-    copies = [pltpu.make_async_copy(head_ref.at[c], heads.at[c], arrived.at[c]) for c in range(own)]
-    for copy in copies:
-        copy.start()
+    split = low_ref.shape[1]
+    joined[:half] = near_ref[...]
+    joined[half:] = far_ref[...]
     for c in range(own):
-        copies[c].wait()
-        for flip, ref in ((0, near_ref), (1, far_ref)):
-            decoded = dot(ref[...], heads[c]) + bias_ref[c : c + 1, :]
-            for step in range(half // per):
-                owner = jnp.bitwise_xor(me, 2 * step + flip)
-                line[owner, :, c, :] = decoded[step * per : (step + 1) * per, :]
-    for owner in range(2 * half // per):
-        out_ref[owner] = line[owner].astype(BF16)
+        value = dot(joined[:, :split], low_ref[c]) + dot(joined[:, split:], high_ref[c])
+        decoded[c] = (value + bias_ref[c : c + 1, :]).astype(BF16)
+    for flip in range(2):
+        for step in range(half // per):
+            owner = jnp.bitwise_xor(me, 2 * step + flip)
+            top = flip * half + step * per
+            out_ref[owner] = jnp.swapaxes(decoded[:, top : top + per, :], 0, 1)
 
 
 def flipped(value, axis, count, flip):
@@ -285,13 +314,12 @@
 
 
 def spread_rows(value, axis, count):
-    near = [value] + [flipped(value, axis, count, 2 * k) for k in range(1, count // 2)]
+    across = flipped(value, axis, count, count // 2)
+    near = []
+    for rows in (value, across):
+        near += [rows] + [flipped(rows, axis, count, 2 * k) for k in range(1, count // 4)]
     near = jnp.concatenate(near, axis=0)
     return near, flipped(near, axis, count, 1)
-
-
-def whole(value):
-    return jax.ShapeDtypeStruct(value[0], value[1])
 
 
 def shards(
@@ -340,7 +368,7 @@
             head_weight,
             head_bias,
         )
-    vmem = pltpu.CompilerParams(vmem_limit_bytes=48 << 20)
+    vmem = pltpu.CompilerParams(vmem_limit_bytes=24 << 20)
     place = jnp.stack([lax.axis_index("loc"), lax.axis_index("chan")]).astype(jnp.int32)
 
     packed = pl.pallas_call(
@@ -351,26 +379,22 @@
         compiler_params=vmem,
         name="pack",
     )(pixels.reshape(peers, pair_rows, pixel_count), patch_mask.T, agg_weight.reshape(1, own))
+    packed, sent_weight, sent_embed = lax.optimization_barrier((packed, embed_weight, chan_embed))
+    packed = lax.all_to_all(packed, "chan", split_axis=0, concat_axis=0, tiled=True)
     sections = [embed_weight]
     for step in range(1, blocks):
         hop = [(i, (i - step) % blocks) for i in range(blocks)]
-        sections.append(lax.ppermute(embed_weight, "loc", hop))
-    near, far = spread_rows(chan_embed, "chan", peers)
-    packed = lax.all_to_all(packed, "chan", split_axis=0, concat_axis=0, tiled=True)
-
-    over = jnp.max((packed[:, rows - 1, :LANES].astype(F32) >= 2.0).astype(jnp.int32))
-    over = jnp.broadcast_to(over, (8, LANES))
-    most = over
-    for step in range(1, blocks):
-        hop = [(i, (i - step) % blocks) for i in range(blocks)]
-        most = jnp.maximum(most, lax.ppermute(over, "loc", hop))
-
+        sections.append(lax.ppermute(sent_weight, "loc", hop))
+    near, far = spread_rows(sent_embed, "chan", peers)
     chunk = 512
-    joined = pl.pallas_call(
+    joined, over = pl.pallas_call(
         functools.partial(join_kernel, (peers, own, per, heads, chunk)),
-        out_shape=jax.ShapeDtypeStruct((per, features), BF16),
-        in_specs=[pl.BlockSpec(memory_space=pltpu.SMEM)] + [VMEM] * (8 + blocks),
-        out_specs=VMEM,
+        out_shape=(
+            jax.ShapeDtypeStruct((per, features), BF16),
+            jax.ShapeDtypeStruct((8, LANES), jnp.int32),
+        ),
+        in_specs=[SMEM] + [VMEM] * (8 + blocks),
+        out_specs=(VMEM, VMEM),
         scratch_shapes=[
             pltpu.VMEM((pixel_count, features), BF16),
             pltpu.VMEM((channels, features), BF16),
@@ -394,9 +418,49 @@
         group_bias,
         norm_gain.reshape(1, features),
     )
-    joined = lax.cond(
-        most[0, 0] > 0,
-        lambda: plain_join(
+    most = [over]
+    for step in range(1, blocks):
+        hop = [(i, (i - step) % blocks) for i in range(blocks)]
+        most.append(lax.ppermute(over, "loc", hop))
+    split = features // 2
+
+    def by_channel(start):
+        block = 256
+        return pl.pallas_call(
+            functools.partial(by_channel_kernel, start),
+            out_shape=jax.ShapeDtypeStruct((own, split, pixel_count), BF16),
+            in_specs=[ANY],
+            out_specs=VMEM,
+            scratch_shapes=[
+                pltpu.VMEM((2, block, own, pixel_count), BF16),
+                pltpu.SemaphoreType.DMA((2,)),
+            ],
+            compiler_params=vmem,
+            cost_estimate=pl.CostEstimate(flops=0, bytes_accessed=4 * own * split * pixel_count, transcendentals=0),
+            name="by_channel",
+        )(sent_head)
+
+    joined, sent_head = lax.optimization_barrier((joined, head_weight))
+    parts = [by_channel(start) for start in range(0, features, split)]
+    near, far = spread_rows(joined, "chan", peers)
+    rebuilt, over = pl.pallas_call(
+        decode_kernel,
+        out_shape=(
+            jax.ShapeDtypeStruct((peers, per, own, pixel_count), BF16),
+            jax.ShapeDtypeStruct((1,), jnp.int32),
+        ),
+        in_specs=[SMEM] + [VMEM] * (5 + blocks),
+        out_specs=(VMEM, SMEM),
+        scratch_shapes=[
+            pltpu.VMEM((locations, features), BF16),
+            pltpu.VMEM((own, locations, pixel_count), BF16),
+        ],
+        compiler_params=vmem,
+        name="decode",
+    )(place, near, far, *parts, head_bias, *most)
+    return lax.cond(
+        over[0] > 0,
+        lambda: plain_shards(
             pixels,
             patch_mask,
             group_map,
@@ -407,25 +471,11 @@
             query_key,
             group_bias,
             norm_gain,
+            head_weight,
+            head_bias,
         ),
-        lambda: joined,
+        lambda: rebuilt.reshape(locations, own, pixel_count),
     )
-    near, far = spread_rows(joined, "chan", peers)
-    by_channel = jnp.transpose(head_weight, (1, 0, 2))
-    rebuilt = pl.pallas_call(
-        decode_kernel,
-        out_shape=jax.ShapeDtypeStruct((peers, per, own, pixel_count), BF16),
-        in_specs=[pl.BlockSpec(memory_space=pltpu.SMEM), VMEM, VMEM, ANY, VMEM],
-        out_specs=VMEM,
-        scratch_shapes=[
-            pltpu.VMEM((own, features, pixel_count), BF16),
-            pltpu.VMEM((peers, per, own, pixel_count), F32),
-            pltpu.SemaphoreType.DMA((own,)),
-        ],
-        compiler_params=vmem,
-        name="decode",
-    )(place, near, far, by_channel, head_bias)
-    return rebuilt.reshape(locations, own, pixel_count)
 
 
 def solution(mesh):

time: 121 us -> 81.4 us (0.67)
  local copies, waits for them, and re-layouts: 19.3 us -> 1.67 us
  between operations: 14.2 us -> 1.09 us
  starting transfers between devices: 38 us -> 30.5 us
  Pallas kernels: 27.7 us -> 31.6 us
  waiting for transfers between devices: 18.7 us -> 15.8 us
  other arithmetic: 1.37 us -> 0.07 us
    unnamed x21 -> x28, local copies, waits for them, and re-layouts: 17.5 us -> 0.96 us
    ppermute x16, starting transfers between devices: 29.9 us -> 23.5 us  [flipped(): return lax.ppermute(value, axis, [(i, i ^ flip) for i in range(count)])]
    pallas_call x1 -> x3, Pallas kernels: 12.6 us -> 17 us  [the longest x2 10 us: by_channel(): pl.pallas_call(functools.partial(by_channel_kernel, start), out_shape=jax...]
    ppermute x16, waiting for transfers between devices: 18.7 us -> 15.2 us  [flipped(): return lax.ppermute(value, axis, [(i, i ^ flip) for i in range(count)])]
  transfers between devices with their start and end apart: 19 -> 19, of which waited for: 4 -> 9; matrix products, arithmetic and copies ran while one was open for 16% -> 2% of each run, Pallas kernels for 13% -> 12%
where the time goes in v1:
time: 81.4 us; the launch traced here: 81 us
  Pallas kernels  31.6 us (39%)
  starting transfers between devices  30.5 us (37%)
  waiting for transfers between devices  15.8 us (19%)
  local copies, waits for them, and re-layouts  1.67 us (2%)
  between operations  1.09 us (1%)
    ppermute x16, starting transfers between devices, flipped(): return lax.ppermute(value, axis, [(i, i ^ flip) for i in range(count)])  23.5 us
    ppermute x16, waiting for transfers between devices, flipped(): return lax.ppermute(value, axis, [(i, i ^ flip) for i in range(count)])  15.2 us
    pallas_call x1, Pallas kernels, shards(): pl.pallas_call(functools.partial(join_kernel, (peers, own, per, heads, ch...  11.3 us
    pallas_call x2, Pallas kernels, by_channel(): pl.pallas_call(functools.partial(by_channel_kernel, start), out_shape=jax...  10 us
    pallas_call x1, Pallas kernels, shards(): pl.pallas_call(decode_kernel, out_shape=(jax.ShapeDtypeStruct((peers, per...  6.93 us
    all_to_all x1, starting transfers between devices, shards(): lax.all_to_all(packed, 'chan', split_axis=0, concat_axis=0, tiled=True)  3.91 us
    pallas_call x1, Pallas kernels, shards(): pl.pallas_call(functools.partial(pack_kernel, rows), out_shape=jax.ShapeD...  3.3 us
  transfers between devices with their start and end apart: 19, of which 9 were waited for; matrix products, arithmetic and copies ran while one was open for 2% of the time, Pallas kernels for 12%

profile of v1, /device:TPU:0, one launch (start us, length us, event | category | flops | bytes accessed | tf_op | source)
XLA Modules:
  0.0 81.0 jit_solution(11352448337569756830)
XLA Ops:
  0.0 3.3 %pack.1 = bf16[16,96,256]{2,1,0:T(8,128)(2,1)} custom-call(bf16[16,256,256]{2,1,0:T(8,128)(2,1)} %bitcast.25.pixels_ref, s32[16,256]{1,0:T(8,128)} %bitcast.99, f32[1,16]{1,0:T(1,128)} %bitcast.105), custom_call_target="tpu_custom_call" | custom-call | tf_op jit(solution)/shard_map/pack/pallas_call | solution.py:374
  3.3 3.0 %collective-permute-start.1 = (bf16[16,2048]{1,0:T(8,128)(2,1)}, bf16[16,2048]{1,0:T(8,128)(2,1)S(1)}, u32[]{:S(2)}, u32[]{:S(2)}) collective-permute-start(bf16[16,2048]{1,0:T(8,128)(2,1)} %param.19), channel_id=1, source_target_pairs={{0,4},{2,6},{4,0},{6,2},{8,12},{10,14},{12,8},{14,10},{16,20},{18,... | collective-permute-start | bytes 196616 | tf_op jit(solution)/shard_map/ppermute | solution.py:313
  6.3 1.6 %collective-permute-start.2 = (bf16[16,2048]{1,0:T(8,128)(2,1)}, bf16[16,2048]{1,0:T(8,128)(2,1)S(1)}, u32[]{:S(2)}, u32[]{:S(2)}) collective-permute-start(bf16[16,2048]{1,0:T(8,128)(2,1)} %param.19), channel_id=1, source_target_pairs={{0,8},{2,10},{4,12},{6,14},{8,0},{10,2},{12,4},{14,6},{16,24},{18,... | collective-permute-start | bytes 196616 | tf_op jit(solution)/shard_map/ppermute | solution.py:313
  7.8 3.0 %collective-permute-start.4 = (bf16[16,2048]{1,0:T(8,128)(2,1)}, bf16[16,2048]{1,0:T(8,128)(2,1)S(1)}, u32[]{:S(2)}, u32[]{:S(2)}) collective-permute-start(bf16[16,2048]{1,0:T(8,128)(2,1)} %param.19), channel_id=1, source_target_pairs={{0,16},{2,18},{4,20},{6,22},{8,24},{10,26},{12,28},{14,30},{16,0},... | collective-permute-start | bytes 196616 | tf_op jit(solution)/shard_map/ppermute | solution.py:313
  10.8 3.9 %all-to-all-start.6 = ((bf16[16,96,256]{2,1,0:T(8,128)(2,1)}), bf16[16,96,256]{2,1,0:T(8,128)(2,1)S(1)}, u32[]{:S(2)}, u32[]{:S(2)}) async-start(bf16[16,96,256]{2,1,0:T(8,128)(2,1)} %pack.1), calls=%async_computation.6 | async-start | bytes 1572864 | tf_op jit(solution)/shard_map/all_to_all | solution.py:383
  14.7 1.6 %collective-permute-start = (bf16[256,1024]{1,0:T(8,128)(2,1)}, bf16[256,1024]{1,0:T(8,128)(2,1)S(1)}, u32[]{:S(2)}, u32[]{:S(2)}) collective-permute-start(bf16[256,1024]{1,0:T(8,128)(2,1)} %refs_0_.1), channel_id=1, source_target_pairs={{0,1},{1,0},{2,3},{3,2},{4,5},{5,4},{6,7},{7,6},{8,9},{9,8},{10,11... | collective-permute-start | bytes 1572872 | tf_op jit(solution)/shard_map/ppermute | solution.py:387
  17.2 1.9 %collective-permute-start.5 = (bf16[16,2048]{1,0:T(8,128)(2,1)S(1)}, bf16[16,2048]{1,0:T(8,128)(2,1)S(1)}, u32[]{:S(2)}, u32[]{:S(2)}) collective-permute-start(bf16[16,2048]{1,0:T(8,128)(2,1)S(1)} %collective-permute-done.4), channel_id=1, source_target_pairs={{0,4},{2,6},{4,0},{6,2},{8,12},{10,14},{12,8},{14,10},{16,20},{18,... | collective-permute-start | bytes 196616 | tf_op jit(solution)/shard_map/ppermute | solution.py:313
  19.0 1.5 %collective-permute-start.6 = (bf16[16,2048]{1,0:T(8,128)(2,1)S(1)}, bf16[16,2048]{1,0:T(8,128)(2,1)S(1)}, u32[]{:S(2)}, u32[]{:S(2)}) collective-permute-start(bf16[16,2048]{1,0:T(8,128)(2,1)S(1)} %collective-permute-done.4), channel_id=1, source_target_pairs={{0,8},{2,10},{4,12},{6,14},{8,0},{10,2},{12,4},{14,6},{16,24},{18,... | collective-permute-start | bytes 196616 | tf_op jit(solution)/shard_map/ppermute | solution.py:313
  20.8 3.3 %collective-permute-done.5 = bf16[16,2048]{1,0:T(8,128)(2,1)S(1)} collective-permute-done((bf16[16,2048]{1,0:T(8,128)(2,1)S(1)}, bf16[16,2048]{1,0:T(8,128)(2,1)S(1)}, u32[]{:S(2)}, u32[]{:S(2)}) %collective-permute-start.5) | collective-permute-done | bytes 65568 | tf_op jit(solution)/shard_map/ppermute | solution.py:313
  24.1 6.2 %collective-permute-done.6 = bf16[16,2048]{1,0:T(8,128)(2,1)S(1)} collective-permute-done((bf16[16,2048]{1,0:T(8,128)(2,1)S(1)}, bf16[16,2048]{1,0:T(8,128)(2,1)S(1)}, u32[]{:S(2)}, u32[]{:S(2)}) %collective-permute-start.6) | collective-permute-done | bytes 65568 | tf_op jit(solution)/shard_map/ppermute | solution.py:313
  30.3 1.0 %collective-permute-done.7 = bf16[16,2048]{1,0:T(8,128)(2,1)S(1)} collective-permute-done((bf16[16,2048]{1,0:T(8,128)(2,1)S(1)}, bf16[16,2048]{1,0:T(8,128)(2,1)S(1)}, u32[]{:S(2)}, u32[]{:S(2)}) %collective-permute-start.7) | collective-permute-done | bytes 65568 | tf_op jit(solution)/shard_map/ppermute | solution.py:313
  32.1 1.1 %collective-permute-done.8.refs_3_ = bf16[128,2048]{1,0:T(8,128)(2,1)S(1)} collective-permute-done((bf16[128,2048]{1,0:T(8,128)(2,1)S(1)}, bf16[128,2048]{1,0:T(8,128)(2,1)S(1)}, u32[]{:S(2)}, u32[]{:S(2)}) %collective-permute-start.8) | collective-permute-done | bytes 524320 | tf_op jit(solution)/shard_map/ppermute | solution.py:313
  33.8 11.3 %join.1 = (bf16[16,2048]{1,0:T(8,128)(2,1)S(1)}, s32[8,128]{1,0:T(8,128)S(1)}) custom-call(s32[2]{0:T(128)S(1)} %pad_add_fusion.1.place_ref, bf16[16,96,256]{2,1,0:T(8,128)(2,1)S(1)} %all-to-all-done.6.packed_ref, bf16[256,1024]{1,0:T(8,128)(2,1)} %refs_0_.1, bf16[256,1024]{1,0:T(8,128)(2,1)S(1)} %collective-permute-done.refs_1_, ...), custom_call_target="tpu_custom_call" | custom-call | tf_op jit(solution)/shard_map/join/pallas_call | solution.py:390
  45.2 1.1 %collective-permute-start.9 = (bf16[16,2048]{1,0:T(8,128)(2,1)S(1)}, bf16[16,2048]{1,0:T(8,128)(2,1)S(1)}, u32[]{:S(2)}, u32[]{:S(2)}) collective-permute-start(bf16[16,2048]{1,0:T(8,128)(2,1)S(1)} %get-tuple-element.58), channel_id=1, source_target_pairs={{0,4},{2,6},{4,0},{6,2},{8,12},{10,14},{12,8},{14,10},{16,20},{18,... | collective-permute-start | bytes 196616 | tf_op jit(solution)/shard_map/ppermute | solution.py:313
  46.2 4.4 %collective-permute-start.12 = (bf16[16,2048]{1,0:T(8,128)(2,1)S(1)}, bf16[16,2048]{1,0:T(8,128)(2,1)S(1)}, u32[]{:S(2)}, u32[]{:S(2)}) collective-permute-start(bf16[16,2048]{1,0:T(8,128)(2,1)S(1)} %get-tuple-element.58), channel_id=1, source_target_pairs={{0,16},{2,18},{4,20},{6,22},{8,24},{10,26},{12,28},{14,30},{16,0},... | collective-permute-start | bytes 196616 | tf_op jit(solution)/shard_map/ppermute | solution.py:313
  50.7 3.4 %collective-permute-start.11 = (bf16[16,2048]{1,0:T(8,128)(2,1)S(1)}, bf16[16,2048]{1,0:T(8,128)(2,1)S(1)}, u32[]{:S(2)}, u32[]{:S(2)}) collective-permute-start(bf16[16,2048]{1,0:T(8,128)(2,1)S(1)} %get-tuple-element.58), channel_id=1, source_target_pairs={{0,12},{2,14},{4,8},{6,10},{8,4},{10,6},{12,0},{14,2},{16,28},{18,... | collective-permute-start | bytes 196616 | tf_op jit(solution)/shard_map/ppermute | solution.py:313
  54.5 1.5 %collective-permute-start.13 = (bf16[16,2048]{1,0:T(8,128)(2,1)S(1)}, bf16[16,2048]{1,0:T(8,128)(2,1)S(1)}, u32[]{:S(2)}, u32[]{:S(2)}) collective-permute-start(bf16[16,2048]{1,0:T(8,128)(2,1)S(1)} %collective-permute-done.12), channel_id=1, source_target_pairs={{0,4},{2,6},{4,0},{6,2},{8,12},{10,14},{12,8},{14,10},{16,20},{18,... | collective-permute-start | bytes 196616 | tf_op jit(solution)/shard_map/ppermute | solution.py:313
  56.0 2.0 %collective-permute-start.15 = (bf16[16,2048]{1,0:T(8,128)(2,1)S(1)}, bf16[16,2048]{1,0:T(8,128)(2,1)S(1)}, u32[]{:S(2)}, u32[]{:S(2)}) collective-permute-start(bf16[16,2048]{1,0:T(8,128)(2,1)S(1)} %collective-permute-done.12), channel_id=1, source_target_pairs={{0,12},{2,14},{4,8},{6,10},{8,4},{10,6},{12,0},{14,2},{16,28},{18,... | collective-permute-start | bytes 196616 | tf_op jit(solution)/shard_map/ppermute | solution.py:313
  58.0 1.9 %collective-permute-done.13 = bf16[16,2048]{1,0:T(8,128)(2,1)S(1)} collective-permute-done((bf16[16,2048]{1,0:T(8,128)(2,1)S(1)}, bf16[16,2048]{1,0:T(8,128)(2,1)S(1)}, u32[]{:S(2)}, u32[]{:S(2)}) %collective-permute-start.13) | collective-permute-done | bytes 65568 | tf_op jit(solution)/shard_map/ppermute | solution.py:313
  60.3 0.9 %collective-permute-done.15 = bf16[16,2048]{1,0:T(8,128)(2,1)S(1)} collective-permute-done((bf16[16,2048]{1,0:T(8,128)(2,1)S(1)}, bf16[16,2048]{1,0:T(8,128)(2,1)S(1)}, u32[]{:S(2)}, u32[]{:S(2)}) %collective-permute-start.15) | collective-permute-done | bytes 65568 | tf_op jit(solution)/shard_map/ppermute | solution.py:313
  61.2 1.6 %collective-permute-start.17 = (s32[8,128]{1,0:T(8,128)S(1)}, s32[8,128]{1,0:T(8,128)S(1)}, u32[]{:S(2)}, u32[]{:S(2)}) collective-permute-start(s32[8,128]{1,0:T(8,128)S(1)} %get-tuple-element.60.refs_0_), channel_id=1, source_target_pairs={{0,1},{1,0},{2,3},{3,2},{4,5},{5,4},{6,7},{7,6},{8,9},{9,8},{10,11... | collective-permute-start | bytes 12296 | tf_op jit(solution)/shard_map/ppermute | solution.py:424
  62.8 5.0 %by_channel.2.low_ref = bf16[16,1024,256]{2,1,0:T(8,128)(2,1)S(1)} custom-call(bf16[2048,16,256]{2,1,0:T(8,128)(2,1)} %head_ref.1), custom_call_target="tpu_custom_call" | custom-call | bytes 16777216 | tf_op jit(solution)/shard_map/by_channel/pallas_call | solution.py:429
  67.9 5.0 %by_channel.3.high_ref = bf16[16,1024,256]{2,1,0:T(8,128)(2,1)S(1)} custom-call(bf16[2048,16,256]{2,1,0:T(8,128)(2,1)} %head_ref.1), custom_call_target="tpu_custom_call" | custom-call | bytes 16777216 | tf_op jit(solution)/shard_map/by_channel/pallas_call | solution.py:429
  72.9 6.9 %decode.1 = (bf16[16,16,16,256]{3,2,1,0:T(8,128)(2,1)}, s32[1]{0:T(128)}) custom-call(s32[2]{0:T(128)S(1)} %pad_add_fusion.1.place_ref, bf16[128,2048]{1,0:T(8,128)(2,1)S(1)} %constant_dynamic-update-slice_fusion.8.near_ref, bf16[128,2048]{1,0:T(8,128)(2,1)S(1)} %collective-permute-done.16.far_ref, bf16[16,1024,256]{2,1,0:T(8,128)(2,1)S(1)} %by_channel.2.low_ref, ...), custom_call_target="tpu_custom_call" | custom-call | tf_op jit(solution)/shard_map/decode/pallas_call | solution.py:446
  (52 shorter events, 3.6 us)
Async XLA Ops:
  3.3 15.7 %collective-permute-start.1 = (bf16[16,2048]{1,0:T(8,128)(2,1)}, bf16[16,2048]{1,0:T(8,128)(2,1)S(1)}, u32[]{:S(2)}, u32[]{:S(2)}) collective-permute-start(bf16[16,2048]{1,0:T(8,128)(2,1)} %param.19), channel_id=1, source_target_pairs={{0,4},{2,6},{4,0},{6,2},{8,12},{10,14},{12,8},{14,10},{16,20},{18,... | collective-permute-start | bytes 196616 | tf_op jit(solution)/shard_map/ppermute | solution.py:313
  6.3 14.2 %collective-permute-start.2 = (bf16[16,2048]{1,0:T(8,128)(2,1)}, bf16[16,2048]{1,0:T(8,128)(2,1)S(1)}, u32[]{:S(2)}, u32[]{:S(2)}) collective-permute-start(bf16[16,2048]{1,0:T(8,128)(2,1)} %param.19), channel_id=1, source_target_pairs={{0,8},{2,10},{4,12},{6,14},{8,0},{10,2},{12,4},{14,6},{16,24},{18,... | collective-permute-start | bytes 196616 | tf_op jit(solution)/shard_map/ppermute | solution.py:313
  7.8 12.9 %collective-permute-start.3 = (bf16[16,2048]{1,0:T(8,128)(2,1)}, bf16[16,2048]{1,0:T(8,128)(2,1)S(1)}, u32[]{:S(2)}, u32[]{:S(2)}) collective-permute-start(bf16[16,2048]{1,0:T(8,128)(2,1)} %param.19), channel_id=1, source_target_pairs={{0,12},{2,14},{4,8},{6,10},{8,4},{10,6},{12,0},{14,2},{16,28},{18,... | collective-permute-start | bytes 196616 | tf_op jit(solution)/shard_map/ppermute | solution.py:313
  7.8 9.3 %collective-permute-start.4 = (bf16[16,2048]{1,0:T(8,128)(2,1)}, bf16[16,2048]{1,0:T(8,128)(2,1)S(1)}, u32[]{:S(2)}, u32[]{:S(2)}) collective-permute-start(bf16[16,2048]{1,0:T(8,128)(2,1)} %param.19), channel_id=1, source_target_pairs={{0,16},{2,18},{4,20},{6,22},{8,24},{10,26},{12,28},{14,30},{16,0},... | collective-permute-start | bytes 196616 | tf_op jit(solution)/shard_map/ppermute | solution.py:313
  10.8 23.0 %all-to-all-start.6 = ((bf16[16,96,256]{2,1,0:T(8,128)(2,1)}), bf16[16,96,256]{2,1,0:T(8,128)(2,1)S(1)}, u32[]{:S(2)}, u32[]{:S(2)}) async-start(bf16[16,96,256]{2,1,0:T(8,128)(2,1)} %pack.1), calls=%async_computation.6 | async-start | bytes 1572864 | tf_op jit(solution)/shard_map/all_to_all | solution.py:383
  14.7 17.3 %collective-permute-start = (bf16[256,1024]{1,0:T(8,128)(2,1)}, bf16[256,1024]{1,0:T(8,128)(2,1)S(1)}, u32[]{:S(2)}, u32[]{:S(2)}) collective-permute-start(bf16[256,1024]{1,0:T(8,128)(2,1)} %refs_0_.1), channel_id=1, source_target_pairs={{0,1},{1,0},{2,3},{3,2},{4,5},{5,4},{6,7},{7,6},{8,9},{9,8},{10,11... | collective-permute-start | bytes 1572872 | tf_op jit(solution)/shard_map/ppermute | solution.py:387
  17.2 6.9 %collective-permute-start.5 = (bf16[16,2048]{1,0:T(8,128)(2,1)S(1)}, bf16[16,2048]{1,0:T(8,128)(2,1)S(1)}, u32[]{:S(2)}, u32[]{:S(2)}) collective-permute-start(bf16[16,2048]{1,0:T(8,128)(2,1)S(1)} %collective-permute-done.4), channel_id=1, source_target_pairs={{0,4},{2,6},{4,0},{6,2},{8,12},{10,14},{12,8},{14,10},{16,20},{18,... | collective-permute-start | bytes 196616 | tf_op jit(solution)/shard_map/ppermute | solution.py:313
  19.0 11.3 %collective-permute-start.6 = (bf16[16,2048]{1,0:T(8,128)(2,1)S(1)}, bf16[16,2048]{1,0:T(8,128)(2,1)S(1)}, u32[]{:S(2)}, u32[]{:S(2)}) collective-permute-start(bf16[16,2048]{1,0:T(8,128)(2,1)S(1)} %collective-permute-done.4), channel_id=1, source_target_pairs={{0,8},{2,10},{4,12},{6,14},{8,0},{10,2},{12,4},{14,6},{16,24},{18,... | collective-permute-start | bytes 196616 | tf_op jit(solution)/shard_map/ppermute | solution.py:313
  20.5 10.8 %collective-permute-start.7 = (bf16[16,2048]{1,0:T(8,128)(2,1)S(1)}, bf16[16,2048]{1,0:T(8,128)(2,1)S(1)}, u32[]{:S(2)}, u32[]{:S(2)}) collective-permute-start(bf16[16,2048]{1,0:T(8,128)(2,1)S(1)} %collective-permute-done.4), channel_id=1, source_target_pairs={{0,12},{2,14},{4,8},{6,10},{8,4},{10,6},{12,0},{14,2},{16,28},{18,... | collective-permute-start | bytes 196616 | tf_op jit(solution)/shard_map/ppermute | solution.py:313
  31.3 1.9 %collective-permute-start.8 = (bf16[128,2048]{1,0:T(8,128)(2,1)S(1)}, bf16[128,2048]{1,0:T(8,128)(2,1)S(1)}, u32[]{:S(2)}, u32[]{:S(2)}) collective-permute-start(bf16[128,2048]{1,0:T(8,128)(2,1)S(1)} %constant_dynamic-update-slice_fusion.refs_2_), channel_id=1, source_target_pairs={{0,2},{2,0},{4,6},{6,4},{8,10},{10,8},{12,14},{14,12},{16,18},{18,... | collective-permute-start | bytes 1572872 | tf_op jit(solution)/shard_map/ppermute | solution.py:313
  45.2 10.9 %collective-permute-start.9 = (bf16[16,2048]{1,0:T(8,128)(2,1)S(1)}, bf16[16,2048]{1,0:T(8,128)(2,1)S(1)}, u32[]{:S(2)}, u32[]{:S(2)}) collective-permute-start(bf16[16,2048]{1,0:T(8,128)(2,1)S(1)} %get-tuple-element.58), channel_id=1, source_target_pairs={{0,4},{2,6},{4,0},{6,2},{8,12},{10,14},{12,8},{14,10},{16,20},{18,... | collective-permute-start | bytes 196616 | tf_op jit(solution)/shard_map/ppermute | solution.py:313
  46.2 8.3 %collective-permute-start.12 = (bf16[16,2048]{1,0:T(8,128)(2,1)S(1)}, bf16[16,2048]{1,0:T(8,128)(2,1)S(1)}, u32[]{:S(2)}, u32[]{:S(2)}) collective-permute-start(bf16[16,2048]{1,0:T(8,128)(2,1)S(1)} %get-tuple-element.58), channel_id=1, source_target_pairs={{0,16},{2,18},{4,20},{6,22},{8,24},{10,26},{12,28},{14,30},{16,0},... | collective-permute-start | bytes 196616 | tf_op jit(solution)/shard_map/ppermute | solution.py:313
  50.7 7.3 %collective-permute-start.10 = (bf16[16,2048]{1,0:T(8,128)(2,1)S(1)}, bf16[16,2048]{1,0:T(8,128)(2,1)S(1)}, u32[]{:S(2)}, u32[]{:S(2)}) collective-permute-start(bf16[16,2048]{1,0:T(8,128)(2,1)S(1)} %get-tuple-element.58), channel_id=1, source_target_pairs={{0,8},{2,10},{4,12},{6,14},{8,0},{10,2},{12,4},{14,6},{16,24},{18,... | collective-permute-start | bytes 196616 | tf_op jit(solution)/shard_map/ppermute | solution.py:313
  50.7 7.3 %collective-permute-start.11 = (bf16[16,2048]{1,0:T(8,128)(2,1)S(1)}, bf16[16,2048]{1,0:T(8,128)(2,1)S(1)}, u32[]{:S(2)}, u32[]{:S(2)}) collective-permute-start(bf16[16,2048]{1,0:T(8,128)(2,1)S(1)} %get-tuple-element.58), channel_id=1, source_target_pairs={{0,12},{2,14},{4,8},{6,10},{8,4},{10,6},{12,0},{14,2},{16,28},{18,... | collective-permute-start | bytes 196616 | tf_op jit(solution)/shard_map/ppermute | solution.py:313
  54.5 5.5 %collective-permute-start.13 = (bf16[16,2048]{1,0:T(8,128)(2,1)S(1)}, bf16[16,2048]{1,0:T(8,128)(2,1)S(1)}, u32[]{:S(2)}, u32[]{:S(2)}) collective-permute-start(bf16[16,2048]{1,0:T(8,128)(2,1)S(1)} %collective-permute-done.12), channel_id=1, source_target_pairs={{0,4},{2,6},{4,0},{6,2},{8,12},{10,14},{12,8},{14,10},{16,20},{18,... | collective-permute-start | bytes 196616 | tf_op jit(solution)/shard_map/ppermute | solution.py:313
  56.0 4.3 %collective-permute-start.14 = (bf16[16,2048]{1,0:T(8,128)(2,1)S(1)}, bf16[16,2048]{1,0:T(8,128)(2,1)S(1)}, u32[]{:S(2)}, u32[]{:S(2)}) collective-permute-start(bf16[16,2048]{1,0:T(8,128)(2,1)S(1)} %collective-permute-done.12), channel_id=1, source_target_pairs={{0,8},{2,10},{4,12},{6,14},{8,0},{10,2},{12,4},{14,6},{16,24},{18,... | collective-permute-start | bytes 196616 | tf_op jit(solution)/shard_map/ppermute | solution.py:313
  56.0 5.2 %collective-permute-start.15 = (bf16[16,2048]{1,0:T(8,128)(2,1)S(1)}, bf16[16,2048]{1,0:T(8,128)(2,1)S(1)}, u32[]{:S(2)}, u32[]{:S(2)}) collective-permute-start(bf16[16,2048]{1,0:T(8,128)(2,1)S(1)} %collective-permute-done.12), channel_id=1, source_target_pairs={{0,12},{2,14},{4,8},{6,10},{8,4},{10,6},{12,0},{14,2},{16,28},{18,... | collective-permute-start | bytes 196616 | tf_op jit(solution)/shard_map/ppermute | solution.py:313
  61.2 11.7 %collective-permute-start.16 = (bf16[128,2048]{1,0:T(8,128)(2,1)S(1)}, bf16[128,2048]{1,0:T(8,128)(2,1)S(1)}, u32[]{:S(2)}, u32[]{:S(2)}) collective-permute-start(bf16[128,2048]{1,0:T(8,128)(2,1)S(1)} %constant_dynamic-update-slice_fusion.8.near_ref), channel_id=1, source_target_pairs={{0,2},{2,0},{4,6},{6,4},{8,10},{10,8},{12,14},{14,12},{16,18},{18,... | collective-permute-start | bytes 1572872 | tf_op jit(solution)/shard_map/ppermute | solution.py:313
  61.2 11.7 %collective-permute-start.17 = (s32[8,128]{1,0:T(8,128)S(1)}, s32[8,128]{1,0:T(8,128)S(1)}, u32[]{:S(2)}, u32[]{:S(2)}) collective-permute-start(s32[8,128]{1,0:T(8,128)S(1)} %get-tuple-element.60.refs_0_), channel_id=1, source_target_pairs={{0,1},{1,0},{2,3},{3,2},{4,5},{5,4},{6,7},{7,6},{8,9},{9,8},{10,11... | collective-permute-start | bytes 12296 | tf_op jit(solution)/shard_map/ppermute | solution.py:424
  67.8 12.7 %copy-start = (bf16[256,1024]{1,0:T(8,128)(2,1)S(1)}, bf16[256,1024]{1,0:T(8,128)(2,1)}, u32[]{:S(2)}) copy-start(bf16[256,1024]{1,0:T(8,128)(2,1)} %refs_0_.1) | copy-start | bytes 1572868
  67.8 12.7 %copy-start.2 = (bf16[16,2048]{1,0:T(8,128)(2,1)S(1)}, bf16[16,2048]{1,0:T(8,128)(2,1)}, u32[]{:S(2)}) copy-start(bf16[16,2048]{1,0:T(8,128)(2,1)} %param.19) | copy-start | bytes 196612
  67.8 12.7 %copy-start.3 = (s32[256,16]{0,1:T(8,128)S(1)}, s32[256,16]{0,1:T(8,128)}, u32[]{:S(2)}) copy-start(s32[256,16]{0,1:T(8,128)} %param.15) | copy-start | bytes 49156
  67.8 12.7 %copy-start.9 = (bf16[2048]{0:T(1024)(128)(2,1)S(1)}, bf16[2048]{0:T(1024)(128)(2,1)}, u32[]{:S(2)}) copy-start(bf16[2048]{0:T(1024)(128)(2,1)} %param.18) | copy-start | bytes 12292
  67.8 12.7 %copy-start.10 = (s32[256]{0:T(256)S(1)}, s32[256]{0:T(256)}, u32[]{:S(2)}) copy-start(s32[256]{0:T(256)} %param.16) | copy-start | bytes 3076
  (2 other events, 17.8 us)
